TPU v7x, 256 devices: a whole 4x4x8 slice. The times are simulated.
256 devices in a mesh: span: 8 (over x, y_lo), tile: 32 (over z, y_hi, core).
Axes of the slice: x: 4, y: 4 (y_hi: 2, y_lo: 2; y = y_hi * 2 + y_lo), z: 8, core: 2. Of those that a mesh axis runs over, the one named last changes fastest.
Arguments:
- tokens: bfloat16 [8, 2304, 1536], P('span', 'tile'), may hold values from -6 to 6
- noise_steps: int32 [8], replicated, may hold values from 0 to 7, as said below
- span_mask: int32 [8, 8], replicated, may hold values from 0 to 1, as said below
- modulation: float32 [8, 5, 1536], replicated, may hold values from -3 to 3
- qkv_weight: bfloat16 [768, 9216], P(None, 'span'), may hold values from -1.5 to 1.5
- out_weight: bfloat16 [1536, 1536], P('span'), may hold values from -0.15625 to 0.15625
- head_weight: bfloat16 [768, 128], replicated, may hold values from -0.15625 to 0.15625
- head_bias: float32 [64], replicated, may hold values from -3 to 3
- frame_cache: bfloat16 [2, 64, 48, 16], P(None, 'tile'), may hold values from -6 to 6
- conv_weight: bfloat16 [432, 384], replicated, may hold values from -0.3125 to 0.3125
- conv_bias: float32 [384], replicated, may hold values from -3 to 3
Outputs:
- hidden_out: bfloat16 [8, 2304, 1536], P('span', 'tile')
- decoded_frames: bfloat16 [3, 64, 48, 384], P(None, 'tile', 'span')
Inputs may be any that keep to these rules, and one draw needn't show every extreme that they name: `noise_steps`: span 0, the finishing span, has level 0 and span 8 - 1 has level 7; the others lie in 1 to 7. `span_mask`: 1 on the diagonal, 0 above it, 0 or 1 below it.
All inputs are finite; a program needn't handle non-finite values.
Results may differ from a plain program's by a relative error of at most 0.015.
Values may be sent and summed in bfloat16 or wider, within the bound.
No kernel may reach another device: no remote copies, remote signals or barrier semaphores. Data moves between devices by JAX's collectives and lax.ppermute only.
A program may use at most 128 MiB of HBM per device.

v0:
```python
import jax
import jax.numpy as jnp
from jax import lax
from jax.sharding import PartitionSpec as P

HDIM = 64
LCH = 16
LF = 3
TROW_DEV = 1
TCOL = 24
epsilon = 1e-06
masked_score = -1e30


def with_halo(cells, sides, width):
    for axis, dim in sides:
        count = lax.axis_size(axis)
        ends = count - 1
        head = lax.slice_in_dim(cells, 0, width, axis=dim)
        tail = lax.slice_in_dim(cells, cells.shape[dim] - width, cells.shape[dim], axis=dim)
        cells = jnp.concatenate(
            [
                lax.ppermute(tail, axis, [(i, (i + 1) % count) for i in range(ends)]),
                cells,
                lax.ppermute(head, axis, [((i + 1) % count, i) for i in range(ends)]),
            ],
            axis=dim,
        )
    return cells


def from_root(block, axis, holder):
    block = jnp.where(lax.axis_index(axis) == holder, block, jnp.zeros_like(block))
    return lax.psum(block, axis)


def layer_norm(values):
    centred = values - jnp.mean(values, axis=-1, keepdims=True)
    spread = jnp.mean(centred * centred, axis=-1, keepdims=True)
    return centred * lax.rsqrt(spread + epsilon)


def convolve(padded, kernel, offsets, frame_count, row_count, col_count):
    pieces = []
    for frame_step in range(3):
        for row_step in range(3):
            for col_step in range(3):
                pieces.append(
                    padded[
                        frame_step : frame_step + frame_count,
                        row_step : row_step + row_count,
                        col_step : col_step + col_count,
                    ]
                )
    stacked = jnp.concatenate(pieces, axis=-1)
    product = jnp.dot(
        stacked.reshape(-1, stacked.shape[-1]), kernel, preferred_element_type=jnp.float32
    )
    return (product.reshape(frame_count, row_count, col_count, -1) + offsets).astype(jnp.bfloat16)


def per_device(
    tokens,
    noise_steps,
    span_mask,
    modulation,
    qkv_weight,
    out_weight,
    head_weight,
    head_bias,
    frame_cache,
    conv_weight,
    conv_bias,
):
    span_count = lax.axis_size("span")
    span_index = lax.axis_index("span")
    level_count = modulation.shape[0]
    picked = (noise_steps[:, None] == jnp.arange(level_count)[None, :]).astype(jnp.float32)
    per_span = jnp.einsum("cl,lkd->ckd", picked, modulation, precision=lax.Precision.HIGHEST)
    own_mod = lax.dynamic_index_in_dim(per_span, span_index, 0, keepdims=False)
    residual = tokens[0].astype(jnp.float32)
    tok_rows = residual.shape[0]
    normed = (layer_norm(residual) * (1.0 + own_mod[1]) + own_mod[0]).astype(jnp.bfloat16)
    half_rows = qkv_weight.shape[0]
    local_heads = qkv_weight.shape[1] // (6 * HDIM)
    local_width = local_heads * HDIM
    flat_weight = jnp.transpose(
        qkv_weight.reshape(half_rows, local_heads, 2, 3, HDIM), (0, 2, 3, 1, 4)
    ).reshape(2 * half_rows, 3 * local_width)
    projected = jnp.dot(
        lax.all_gather(normed, "span", axis=0, tiled=True),
        flat_weight,
        preferred_element_type=jnp.float32,
    ).astype(jnp.bfloat16)
    all_rows = projected.shape[0]
    queries = projected[:, :local_width].reshape(all_rows, local_heads, HDIM)
    key_rows = projected[:, local_width : 2 * local_width].reshape(
        span_count, tok_rows, local_width
    )
    value_rows = projected[:, 2 * local_width :].reshape(span_count, tok_rows, local_width)
    seen_spans = jnp.repeat(span_mask > 0, tok_rows, axis=0)
    score_scale = HDIM ** (-0.5)
    start_state = (
        jnp.full((local_heads, all_rows), masked_score, jnp.float32),
        jnp.zeros((local_heads, all_rows), jnp.float32),
        jnp.zeros((all_rows, local_heads, HDIM), jnp.float32),
    )
    key_piece = lax.all_gather(key_rows, "tile", axis=1, tiled=True)
    value_piece = lax.all_gather(value_rows, "tile", axis=1, tiled=True)
    piece_rows = key_piece.shape[1]
    block_rows = piece_rows
    while span_count * block_rows > 2048 and block_rows % 2 == 0:
        block_rows = block_rows // 2
    block_count = piece_rows // block_rows
    block_keys = span_count * block_rows
    key_blocks = jnp.transpose(
        key_piece.reshape(span_count, block_count, block_rows, local_heads, HDIM), (1, 0, 2, 3, 4)
    ).reshape(block_count, block_keys, local_heads, HDIM)
    value_blocks = jnp.transpose(
        value_piece.reshape(span_count, block_count, block_rows, local_heads, HDIM), (1, 0, 2, 3, 4)
    ).reshape(block_count, block_keys, local_heads, HDIM)
    allowed = jnp.repeat(seen_spans, block_rows, axis=1)

    def one_block(running, block_item):
        running_max, running_sum, weighted = running
        key_heads, value_heads = block_item
        scores = (
            jnp.einsum("qhd,khd->hqk", queries, key_heads, preferred_element_type=jnp.float32)
            * score_scale
        )
        scores = jnp.where(allowed[None, :, :], scores, masked_score)
        new_max = jnp.maximum(running_max, jnp.max(scores, axis=-1))
        rescale = jnp.exp(running_max - new_max)
        weights = jnp.where(allowed[None, :, :], jnp.exp(scores - new_max[:, :, None]), 0.0)
        running_sum = running_sum * rescale + jnp.sum(weights, axis=-1)
        blended = jnp.einsum(
            "hqk,khd->qhd",
            weights.astype(jnp.bfloat16),
            value_heads,
            preferred_element_type=jnp.float32,
        )
        weighted = weighted * jnp.transpose(rescale)[:, :, None] + blended
        return ((new_max, running_sum, weighted), None)

    folded, unused = lax.scan(one_block, start_state, (key_blocks, value_blocks))
    final_max, final_sum, final_weighted = folded
    merged = (
        (final_weighted / jnp.transpose(final_sum)[:, :, None])
        .astype(jnp.bfloat16)
        .reshape(all_rows, local_width)
    )
    projected_out = lax.psum_scatter(
        jnp.dot(merged, out_weight, preferred_element_type=jnp.float32).astype(jnp.bfloat16),
        "span",
        scatter_dimension=0,
        tiled=True,
    ).astype(jnp.float32)
    hidden = (residual + own_mod[2] * projected_out).astype(jnp.bfloat16)
    finish_mod = per_span[0]
    shaped = (
        layer_norm(hidden.astype(jnp.float32)) * (1.0 + finish_mod[4]) + finish_mod[3]
    ).astype(jnp.bfloat16)
    head_full = head_weight.reshape(2 * head_weight.shape[0], head_weight.shape[1] // 2)
    patches = (jnp.dot(shaped, head_full, preferred_element_type=jnp.float32) + head_bias).astype(
        jnp.bfloat16
    )
    latent = patches.reshape(LF, TROW_DEV, TCOL, 2, 2, LCH)
    latent = jnp.transpose(latent, (0, 1, 3, 2, 4, 5)).reshape(LF, 2 * TROW_DEV, 2 * TCOL, LCH)
    frames = jnp.concatenate([frame_cache, latent], axis=0)
    padded = with_halo(frames, (("tile", 1),), 1)
    padded = jnp.pad(padded, ((0, 0), (0, 0), (1, 1), (0, 0)))
    strip_rows = 2 * TROW_DEV
    slice_width = 2 * TCOL // span_count
    whole_strip = convolve(padded, conv_weight, conv_bias, LF, strip_rows, 2 * TCOL)
    whole_strip = from_root(whole_strip, "span", 0)
    decoded_frames = lax.dynamic_slice_in_dim(whole_strip, span_index * slice_width, slice_width, 2)
    return (hidden[None], decoded_frames)


def solution(mesh):
    in_specs = (
        P("span", "tile", None),
        P(),
        P(),
        P(),
        P(None, "span"),
        P("span", None),
        P(),
        P(),
        P(None, "tile", None, None),
        P(),
        P(),
    )
    out_specs = (P("span", "tile", None), P(None, "tile", "span", None))
    return jax.shard_map(
        per_device, mesh=mesh, in_specs=in_specs, out_specs=out_specs, check_vma=False
    )
```

profile of v0, /device:TPU:32, one launch (start us, length us, event | category | flops | bytes accessed | tf_op | source)
XLA Modules:
  0.0 755.8 jit_solution(9652505402966992320)
XLA Ops:
  21.1 7.8 %reshape.108 = bf16[1536,576]{1,0:T(8,128)(2,1)S(1)} reshape(bf16[768,2,3,3,64]{4,3,2,1,0:T(4,128)(2,1)} %copy.104) | data formatting | bytes 3538944 | tf_op jit(solution)/shard_map/reshape | solution.py:89
  29.0 35.0 %all-gather.4.cloned.1.call-done = bf16[576,1536]{1,0:T(8,128)(2,1)} async-done(((bf16[72,1536]{1,0:T(8,128)(2,1)}), bf16[576,1536]{1,0:T(8,128)(2,1)}) %all-gather.4.cloned.1.call-update) | async-done | bytes 1769488 | tf_op jit(solution)/shard_map/all_gather | solution.py:91
  69.6 104.5 %all-gather.6.cloned.1.call-done = bf16[8,2304,192]{2,1,0:T(8,128)(2,1)} async-done(((bf16[8,72,192]{2,1,0:T(8,128)(2,1)}), bf16[8,2304,192]{2,1,0:T(8,128)(2,1)}) %all-gather.6.cloned.1.call-update) | async-done | bytes 7077904 | tf_op jit(solution)/shard_map/all_gather | solution.py:108
  174.0 11.4 %copy.106 = bf16[8,2304,192]{1,2,0:T(8,128)(2,1)} copy(bf16[8,2304,192]{2,1,0:T(8,128)(2,1)} %all-gather.6.cloned.1.call-done) | data formatting | bytes 14155776 | tf_op jit(solution)/shard_map/all_gather | solution.py:108
  185.4 23.0 %reshape.110 = bf16[8,16,144,3,64]{2,1,4,3,0:T(8,128)(2,1)} reshape(bf16[8,2304,192]{1,2,0:T(8,128)(2,1)} %copy.106) | data formatting | bytes 14155776 | tf_op jit(solution)/shard_map/reshape | solution.py:117
  208.4 14.1 %copy.107 = bf16[16,8,144,3,64]{2,1,4,3,0:T(8,128)(2,1)} copy(bf16[16,8,144,3,64]{2,0,4,3,1:T(8,128)(2,1)} %bitcast.115) | data formatting | bytes 14155776 | tf_op jit(solution)/shard_map/transpose | solution.py:116
  222.5 19.5 %reshape.111 = bf16[16,1152,3,64]{1,3,2,0:T(8,128)(2,1)} reshape(bf16[16,8,144,3,64]{2,1,4,3,0:T(8,128)(2,1)} %copy.107) | data formatting | bytes 14155776 | tf_op jit(solution)/shard_map/reshape | solution.py:118
  242.0 37.4 %all-gather.8.cloned.1.call-done = bf16[8,2304,192]{2,1,0:T(8,128)(2,1)} async-done(((bf16[8,72,192]{2,1,0:T(8,128)(2,1)}), bf16[8,2304,192]{2,1,0:T(8,128)(2,1)}) %all-gather.8.cloned.1.call-update) | async-done | bytes 7077904 | tf_op jit(solution)/shard_map/all_gather | solution.py:109
  279.5 11.4 %copy.109 = bf16[8,2304,192]{1,2,0:T(8,128)(2,1)} copy(bf16[8,2304,192]{2,1,0:T(8,128)(2,1)} %all-gather.8.cloned.1.call-done) | data formatting | bytes 14155776 | tf_op jit(solution)/shard_map/all_gather | solution.py:109
  290.9 23.0 %reshape.114 = bf16[8,16,144,3,64]{2,1,4,3,0:T(8,128)(2,1)} reshape(bf16[8,2304,192]{1,2,0:T(8,128)(2,1)} %copy.109) | data formatting | bytes 14155776 | tf_op jit(solution)/shard_map/reshape | solution.py:120
  313.9 14.1 %copy.110 = bf16[16,8,144,3,64]{2,1,4,3,0:T(8,128)(2,1)} copy(bf16[16,8,144,3,64]{2,0,4,3,1:T(8,128)(2,1)} %bitcast.116) | data formatting | bytes 14155776 | tf_op jit(solution)/shard_map/transpose | solution.py:119
  327.9 19.3 %reshape.115 = bf16[16,1152,3,64]{1,3,2,0:T(8,128)(2,1)} reshape(bf16[16,8,144,3,64]{2,1,4,3,0:T(8,128)(2,1)} %copy.110) | data formatting | bytes 14155776 | tf_op jit(solution)/shard_map/reshape | solution.py:121
  347.3 258.2 %while.15 = (s32[]{:T(128)}, f32[3,576]{1,0:T(4,128)S(1)}, f32[3,576]{1,0:T(4,128)S(1)}, f32[576,3,64]{0,2,1:T(8,128)S(1)}, bf16[16,1152,3,64]{1,3,2,0:T(8,128)(...) while((s32[]{:T(128)}, f32[3,576]{1,0:T(4,128)S(1)}, ...), condition=%wide.region_5.6_spmd.clone, body=%wide.region_2.5_spmd.clone.sunk | while | flops 535828608 | bytes 61826696 | solution.py:145
  349.1 5.9 fusion.87
  355.0 5.9 fusion.91
  365.3 5.9 fusion.87
  371.1 5.9 fusion.91
  381.4 5.9 fusion.87
  387.3 5.9 fusion.91
  397.5 5.9 fusion.87
  403.4 5.9 fusion.91
  413.6 5.9 fusion.87
  419.5 5.9 fusion.91
  429.8 5.9 fusion.87
  435.7 5.9 fusion.91
  445.9 5.9 fusion.87
  451.8 5.9 fusion.91
  462.0 5.9 fusion.87
  467.9 5.9 fusion.91
  478.1 5.9 fusion.87
  484.0 5.9 fusion.91
  494.3 5.9 fusion.87
  500.2 5.9 fusion.91
  510.4 5.9 fusion.87
  516.3 5.9 fusion.91
  526.5 5.9 fusion.87
  532.4 5.9 fusion.91
  542.6 5.9 fusion.87
  548.5 5.9 fusion.91
  558.8 5.9 fusion.87
  564.7 5.9 fusion.91
  574.9 5.9 fusion.87
  580.8 5.9 fusion.91
  591.0 5.9 fusion.87
  596.9 5.9 fusion.91
  607.9 45.9 %reduce-scatter.2.cloned.1.call-done = bf16[72,1536]{1,0:T(8,128)(2,1)} async-done(((bf16[576,1536]{1,0:T(8,128)(2,1)}), bf16[72,1536]{1,0:T(8,128)(2,1)}) %reduce-scatter.2.cloned.1.call-update) | async-done | bytes 221200 | tf_op jit(solution)/shard_map/reduce_scatter | solution.py:152
  657.7 6.0 collective-permute-start.1
  668.1 79.6 %all-reduce.3.cloned.1.call-done = bf16[3,2,48,384]{3,2,1,0:T(8,128)(2,1)} async-done(((bf16[3,2,48,384]{3,2,1,0:T(8,128)(2,1)}), bf16[3,2,48,384]{3,2,1,0:T(8,128)(2,1)}) %all-reduce.3.cloned.1.call-update) | async-done | bytes 221200 | tf_op jit(solution)/shard_map/psum | solution.py:34
  (200 shorter events, 100.5 us)
Async XLA Ops:
  7.2 598.4 %copy-start = (bf16[192,1536]{1,0:T(8,128)(2,1)S(1)}, bf16[192,1536]{1,0:T(8,128)(2,1)}, u32[]{:S(2)}) copy-start(bf16[192,1536]{1,0:T(8,128)(2,1)} %param.18) | copy-start | bytes 1769476
  7.2 56.9 %all-gather.4.cloned.1.call-start = ((), (), s32[]{:S(2)}) async-start(), calls=%async_computation.1 | async-start | bytes 1990656 | tf_op jit(solution)/shard_map/all_gather | solution.py:91
  12.7 161.3 %all-gather.6.cloned.1.call-start = ((), (), s32[]{:S(2)}) async-start(), calls=%async_computation.2 | async-start | bytes 9732096 | tf_op jit(solution)/shard_map/all_gather | solution.py:108
  29.0 40.3 %copy-start.6 = (s32[8,8]{1,0:T(8,128)S(1)}, s32[8,8]{1,0:T(8,128)}, u32[]{:S(2)}) copy-start(s32[8,8]{1,0:T(8,128)} %param.15) | copy-start | bytes 772
  68.1 211.4 %all-gather.8.cloned.1.call-start = ((), (), s32[]{:S(2)}) async-start(), calls=%async_computation.3 | async-start | bytes 9732096 | tf_op jit(solution)/shard_map/all_gather | solution.py:109
  69.0 584.8 %reduce-scatter.2.cloned.1.call-start = ((), (), s32[]{:S(2)}) async-start(), calls=%async_computation.4 | async-start | bytes 1990656 | tf_op jit(solution)/shard_map/reduce_scatter | solution.py:152
  347.2 260.3 %copy-start.4 = (bf16[768,128]{1,0:T(8,128)(2,1)S(1)}, bf16[768,128]{1,0:T(8,128)(2,1)}, u32[]{:S(2)}) copy-start(bf16[768,128]{1,0:T(8,128)(2,1)} %param.19) | copy-start | bytes 589828
  347.2 260.5 %copy-start.5 = (bf16[2,2,48,16]{2,3,1,0:T(8,128)(2,1)S(1)}, bf16[2,2,48,16]{2,3,1,0:T(8,128)(2,1)}, u32[]{:S(2)}) copy-start(bf16[2,2,48,16]{2,3,1,0:T(8,128)(2,1)} %param.21) | copy-start | bytes 18436
  347.2 306.5 %copy-start.2 = (bf16[1,72,1536]{2,1,0:T(8,128)(2,1)S(1)}, bf16[1,72,1536]{2,1,0:T(8,128)(2,1)}, u32[]{:S(2)}) copy-start(bf16[1,72,1536]{2,1,0:T(8,128)(2,1)} %param.13) | copy-start | bytes 663556
  347.2 307.9 %copy-start.9 = (f32[64]{0:T(128)S(1)}, f32[64]{0:T(128)}, u32[]{:S(2)}) copy-start(f32[64]{0:T(128)} %param.20) | copy-start | bytes 772
  355.0 5.9 copy-start.1
  371.1 5.9 copy-start.1
  387.3 5.9 copy-start.1
  403.4 5.9 copy-start.1
  419.5 5.9 copy-start.1
  435.6 5.9 copy-start.1
  451.8 5.9 copy-start.1
  467.9 5.9 copy-start.1
  484.0 5.9 copy-start.1
  500.1 5.9 copy-start.1
  516.3 5.9 copy-start.1
  532.4 5.9 copy-start.1
  548.5 5.9 copy-start.1
  564.7 5.9 copy-start.1
  580.8 5.9 copy-start.1
  596.9 5.9 copy-start.1
  605.5 61.5 %copy-start.7 = (bf16[432,384]{1,0:T(8,128)(2,1)S(1)}, bf16[432,384]{1,0:T(8,128)(2,1)}, u32[]{:S(2)}) copy-start(bf16[432,384]{1,0:T(8,128)(2,1)} %param.22) | copy-start | bytes 995332
  605.5 61.5 %copy-start.8 = (f32[384]{0:T(512)S(1)}, f32[384]{0:T(512)}, u32[]{:S(2)}) copy-start(f32[384]{0:T(512)} %param.23) | copy-start | bytes 4612
  607.5 140.2 %all-reduce.3.cloned.1.call-start = ((), (), s32[]{:S(2)}) async-start(), calls=%async_computation.5 | async-start | bytes 442368 | tf_op jit(solution)/shard_map/psum | solution.py:34
  654.9 94.4 %copy-start.3 = (bf16[72,1536]{1,0:T(8,128)(2,1)}, bf16[72,1536]{1,0:T(8,128)(2,1)S(1)}, u32[]{:S(2)}) copy-start(bf16[72,1536]{1,0:T(8,128)(2,1)S(1)} %get-tuple-element.115) | copy-start | bytes 663556
  655.8 8.0 %collective-permute-start = (bf16[5,1,48,16]{3,2,1,0:T(8,128)(2,1)S(1)}, bf16[5,1,48,16]{3,2,1,0:T(8,128)(2,1)S(1)}, u32[]{:S(2)}, u32[]{:S(2)}) collective-permute-start(bf16[5,1,48,16]{3,2,1,0:T(8,128)(2,1)S(1)} %get-tuple-element.149), channel_id=1, source_target_pairs={{0,1},{1,2},{2,3},{3,4},{4,5},{5,6},{6,7},{7,8},{8,9},{9,10},{10,1... | collective-permute-start | bytes 23048 | tf_op jit(solution)/shard_map/ppermute | solution.py:23
  657.7 7.9 %collective-permute-start.1 = (bf16[5,1,48,16]{3,2,1,0:T(8,128)(2,1)S(1)}, bf16[5,1,48,16]{3,2,1,0:T(8,128)(2,1)S(1)}, u32[]{:S(2)}, u32[]{:S(2)}) collective-permute-start(bf16[5,1,48,16]{3,2,1,0:T(8,128)(2,1)S(1)} %get-tuple-element.150), channel_id=1, source_target_pairs={{1,0},{2,1},{3,2},{4,3},{5,4},{6,5},{7,6},{8,7},{9,8},{10,9},{11,1... | collective-permute-start | bytes 23048 | tf_op jit(solution)/shard_map/ppermute | solution.py:25
Sparse Core Ops, SparseCore 0:
  12.8 51.1 all-gather.3
  68.2 105.7 all-gather.5
  176.8 102.6 all-gather.7
  607.6 46.1 reduce-scatter.1
  668.2 79.4 all-reduce.2
where the time goes:
time: 760 us; the launch traced here: 756 us
  waiting for transfers between devices  304 us (40%)
  matrix products  195 us (26%)
  local copies, waits for them, and re-layouts  183 us (24%)
  other arithmetic  48.9 us (6%)
  between operations  14.1 us (2%)
  starting transfers between devices  8.35 us (1%)
    all_gather x1, waiting for transfers between devices, per_device(): key_piece = lax.all_gather(key_rows, 'tile', axis=1, tiled=True)  104 us
    dot_general x16, matrix products, one_block(): jnp.einsum('hqk,khd->qhd', weights.astype(jnp.bfloat16), value_heads, pre...  93.9 us
    dot_general x16, matrix products, one_block(): jnp.einsum('qhd,khd->hqk', queries, key_heads, preferred_element_type=jnp...  93.9 us
    psum x1, waiting for transfers between devices, from_root(): return lax.psum(block, axis)  79.6 us
    reduce_scatter x1, waiting for transfers between devices, per_device(): lax.psum_scatter(jnp.dot(merged, out_weight, preferred_element_type=jnp.f...  45.9 us
    reduce_sum x16, other arithmetic, one_block(): running_sum = running_sum * rescale + jnp.sum(weights, axis=-1)  42.6 us
    all_gather x1, waiting for transfers between devices, per_device(): value_piece = lax.all_gather(value_rows, 'tile', axis=1, tiled=True)  37.4 us
    all_gather x1, waiting for transfers between devices, per_device(): lax.all_gather(normed, 'span', axis=0, tiled=True)  35 us
  transfers between devices with their start and end apart: 7, of which 6 were waited for; matrix products, arithmetic and copies ran while one was open for 11% of the time, Pallas kernels for 0%

commit v1 on v0

--- a/solution.py
+++ b/solution.py
@@ -31,7 +31,7 @@
 
 def from_root(block, axis, holder):
     block = jnp.where(lax.axis_index(axis) == holder, block, jnp.zeros_like(block))
-    return lax.psum(block, axis)
+    return jnp.sum(lax.all_gather(block, axis), axis=0)
 
 
 def layer_norm(values):

time: 760 us -> 732 us (0.963)
  waiting for transfers between devices: 304 us -> 275 us
    psum x1 -> x0, waiting for transfers between devices: 79.6 us -> none  [from_root(): return lax.psum(block, axis)]
    all_gather x0 -> x1, waiting for transfers between devices: none -> 50.5 us  [from_root(): return jnp.sum(lax.all_gather(block, axis), axis=0)]
  transfers between devices with their start and end apart: 7 -> 7, of which waited for: 6 -> 6; matrix products, arithmetic and copies ran while one was open for 11% -> 12% of each run, Pallas kernels for 0% -> 0%
where the time goes in v1:
time: 732 us; the launch traced here: 728 us
  waiting for transfers between devices  275 us (38%)
  matrix products  195 us (27%)
  local copies, waits for them, and re-layouts  183 us (25%)
  other arithmetic  50.7 us (7%)
  between operations  14.1 us (2%)
  starting transfers between devices  8.35 us (1%)
    all_gather x1, waiting for transfers between devices, per_device(): key_piece = lax.all_gather(key_rows, 'tile', axis=1, tiled=True)  104 us
    dot_general x16, matrix products, one_block(): jnp.einsum('hqk,khd->qhd', weights.astype(jnp.bfloat16), value_heads, pre...  93.9 us
    dot_general x16, matrix products, one_block(): jnp.einsum('qhd,khd->hqk', queries, key_heads, preferred_element_type=jnp...  93.9 us
    all_gather x1, waiting for transfers between devices, from_root(): return jnp.sum(lax.all_gather(block, axis), axis=0)  50.5 us
    reduce_scatter x1, waiting for transfers between devices, per_device(): lax.psum_scatter(jnp.dot(merged, out_weight, preferred_element_type=jnp.f...  45.9 us
    reduce_sum x16, other arithmetic, one_block(): running_sum = running_sum * rescale + jnp.sum(weights, axis=-1)  42.6 us
    all_gather x1, waiting for transfers between devices, per_device(): value_piece = lax.all_gather(value_rows, 'tile', axis=1, tiled=True)  37.4 us
    all_gather x1, waiting for transfers between devices, per_device(): lax.all_gather(normed, 'span', axis=0, tiled=True)  35 us
  transfers between devices with their start and end apart: 7, of which 6 were waited for; matrix products, arithmetic and copies ran while one was open for 12% of the time, Pallas kernels for 0%

profile of v1, /device:TPU:32, one launch (start us, length us, event | category | flops | bytes accessed | tf_op | source)
XLA Modules:
  0.0 727.6 jit_solution(1447274559728251920)
XLA Ops:
  21.1 7.8 %reshape.108 = bf16[1536,576]{1,0:T(8,128)(2,1)S(1)} reshape(bf16[768,2,3,3,64]{4,3,2,1,0:T(4,128)(2,1)} %copy.100) | data formatting | bytes 3538944 | tf_op jit(solution)/shard_map/reshape | solution.py:89
  29.0 35.0 %all-gather.6.cloned.1.call-done = bf16[576,1536]{1,0:T(8,128)(2,1)} async-done(((bf16[72,1536]{1,0:T(8,128)(2,1)}), bf16[576,1536]{1,0:T(8,128)(2,1)}) %all-gather.6.cloned.1.call-update) | async-done | bytes 1769488 | tf_op jit(solution)/shard_map/all_gather | solution.py:91
  69.6 104.5 %all-gather.8.cloned.1.call-done = bf16[8,2304,192]{2,1,0:T(8,128)(2,1)} async-done(((bf16[8,72,192]{2,1,0:T(8,128)(2,1)}), bf16[8,2304,192]{2,1,0:T(8,128)(2,1)}) %all-gather.8.cloned.1.call-update) | async-done | bytes 7077904 | tf_op jit(solution)/shard_map/all_gather | solution.py:108
  174.0 11.4 %copy.102 = bf16[8,2304,192]{1,2,0:T(8,128)(2,1)} copy(bf16[8,2304,192]{2,1,0:T(8,128)(2,1)} %all-gather.8.cloned.1.call-done) | data formatting | bytes 14155776 | tf_op jit(solution)/shard_map/all_gather | solution.py:108
  185.4 23.0 %reshape.110 = bf16[8,16,144,3,64]{2,1,4,3,0:T(8,128)(2,1)} reshape(bf16[8,2304,192]{1,2,0:T(8,128)(2,1)} %copy.102) | data formatting | bytes 14155776 | tf_op jit(solution)/shard_map/reshape | solution.py:117
  208.4 14.1 %copy.103 = bf16[16,8,144,3,64]{2,1,4,3,0:T(8,128)(2,1)} copy(bf16[16,8,144,3,64]{2,0,4,3,1:T(8,128)(2,1)} %bitcast.116) | data formatting | bytes 14155776 | tf_op jit(solution)/shard_map/transpose | solution.py:116
  222.5 19.5 %reshape.111 = bf16[16,1152,3,64]{1,3,2,0:T(8,128)(2,1)} reshape(bf16[16,8,144,3,64]{2,1,4,3,0:T(8,128)(2,1)} %copy.103) | data formatting | bytes 14155776 | tf_op jit(solution)/shard_map/reshape | solution.py:118
  242.0 37.4 %all-gather.10.cloned.1.call-done = bf16[8,2304,192]{2,1,0:T(8,128)(2,1)} async-done(((bf16[8,72,192]{2,1,0:T(8,128)(2,1)}), bf16[8,2304,192]{2,1,0:T(8,128)(2,1)}) %all-gather.10.cloned.1.call-update) | async-done | bytes 7077904 | tf_op jit(solution)/shard_map/all_gather | solution.py:109
  279.5 11.4 %copy.105 = bf16[8,2304,192]{1,2,0:T(8,128)(2,1)} copy(bf16[8,2304,192]{2,1,0:T(8,128)(2,1)} %all-gather.10.cloned.1.call-done) | data formatting | bytes 14155776 | tf_op jit(solution)/shard_map/all_gather | solution.py:109
  290.9 23.0 %reshape.114 = bf16[8,16,144,3,64]{2,1,4,3,0:T(8,128)(2,1)} reshape(bf16[8,2304,192]{1,2,0:T(8,128)(2,1)} %copy.105) | data formatting | bytes 14155776 | tf_op jit(solution)/shard_map/reshape | solution.py:120
  313.9 14.1 %copy.106 = bf16[16,8,144,3,64]{2,1,4,3,0:T(8,128)(2,1)} copy(bf16[16,8,144,3,64]{2,0,4,3,1:T(8,128)(2,1)} %bitcast.117) | data formatting | bytes 14155776 | tf_op jit(solution)/shard_map/transpose | solution.py:119
  327.9 19.3 %reshape.115 = bf16[16,1152,3,64]{1,3,2,0:T(8,128)(2,1)} reshape(bf16[16,8,144,3,64]{2,1,4,3,0:T(8,128)(2,1)} %copy.106) | data formatting | bytes 14155776 | tf_op jit(solution)/shard_map/reshape | solution.py:121
  347.3 258.2 %while.15 = (s32[]{:T(128)}, f32[3,576]{1,0:T(4,128)S(1)}, f32[3,576]{1,0:T(4,128)S(1)}, f32[576,3,64]{0,2,1:T(8,128)S(1)}, bf16[16,1152,3,64]{1,3,2,0:T(8,128)(...) while((s32[]{:T(128)}, f32[3,576]{1,0:T(4,128)S(1)}, ...), condition=%wide.region_5.6_spmd.clone, body=%wide.region_2.5_spmd.clone.sunk | while | flops 535828608 | bytes 61826696 | solution.py:145
  349.1 5.9 fusion.87
  355.0 5.9 fusion.91
  365.3 5.9 fusion.87
  371.1 5.9 fusion.91
  381.4 5.9 fusion.87
  387.3 5.9 fusion.91
  397.5 5.9 fusion.87
  403.4 5.9 fusion.91
  413.6 5.9 fusion.87
  419.5 5.9 fusion.91
  429.8 5.9 fusion.87
  435.7 5.9 fusion.91
  445.9 5.9 fusion.87
  451.8 5.9 fusion.91
  462.0 5.9 fusion.87
  467.9 5.9 fusion.91
  478.1 5.9 fusion.87
  484.0 5.9 fusion.91
  494.3 5.9 fusion.87
  500.2 5.9 fusion.91
  510.4 5.9 fusion.87
  516.3 5.9 fusion.91
  526.5 5.9 fusion.87
  532.4 5.9 fusion.91
  542.6 5.9 fusion.87
  548.5 5.9 fusion.91
  558.8 5.9 fusion.87
  564.7 5.9 fusion.91
  574.9 5.9 fusion.87
  580.8 5.9 fusion.91
  591.0 5.9 fusion.87
  596.9 5.9 fusion.91
  607.9 45.9 %reduce-scatter.2.cloned.1.call-done = bf16[72,1536]{1,0:T(8,128)(2,1)} async-done(((bf16[576,1536]{1,0:T(8,128)(2,1)}), bf16[72,1536]{1,0:T(8,128)(2,1)}) %reduce-scatter.2.cloned.1.call-update) | async-done | bytes 221200 | tf_op jit(solution)/shard_map/reduce_scatter | solution.py:152
  657.7 6.0 collective-permute-start.1
  668.1 50.5 %all-gather.12.cloned.1.call-done = bf16[24,2,48,384]{3,2,1,0:T(8,128)(2,1)} async-done(((bf16[3,2,48,384]{3,2,1,0:T(8,128)(2,1)}), bf16[24,2,48,384]{3,2,1,0:T(8,128)(2,1)}) %all-gather.12.cloned.1.call-update) | async-done | bytes 1769488 | tf_op jit(solution)/shard_map/all_gather | solution.py:34
  (201 shorter events, 101.4 us)
Async XLA Ops:
  7.2 598.4 %copy-start = (bf16[192,1536]{1,0:T(8,128)(2,1)S(1)}, bf16[192,1536]{1,0:T(8,128)(2,1)}, u32[]{:S(2)}) copy-start(bf16[192,1536]{1,0:T(8,128)(2,1)} %param.18) | copy-start | bytes 1769476
  7.2 56.9 %all-gather.6.cloned.1.call-start = ((), (), s32[]{:S(2)}) async-start(), calls=%async_computation.1 | async-start | bytes 1990656 | tf_op jit(solution)/shard_map/all_gather | solution.py:91
  12.7 161.3 %all-gather.8.cloned.1.call-start = ((), (), s32[]{:S(2)}) async-start(), calls=%async_computation.2 | async-start | bytes 9732096 | tf_op jit(solution)/shard_map/all_gather | solution.py:108
  29.0 40.3 %copy-start.6 = (s32[8,8]{1,0:T(8,128)S(1)}, s32[8,8]{1,0:T(8,128)}, u32[]{:S(2)}) copy-start(s32[8,8]{1,0:T(8,128)} %param.15) | copy-start | bytes 772
  68.1 211.4 %all-gather.10.cloned.1.call-start = ((), (), s32[]{:S(2)}) async-start(), calls=%async_computation.3 | async-start | bytes 9732096 | tf_op jit(solution)/shard_map/all_gather | solution.py:109
  69.0 584.8 %reduce-scatter.2.cloned.1.call-start = ((), (), s32[]{:S(2)}) async-start(), calls=%async_computation.4 | async-start | bytes 1990656 | tf_op jit(solution)/shard_map/reduce_scatter | solution.py:152
  347.2 260.3 %copy-start.4 = (bf16[768,128]{1,0:T(8,128)(2,1)S(1)}, bf16[768,128]{1,0:T(8,128)(2,1)}, u32[]{:S(2)}) copy-start(bf16[768,128]{1,0:T(8,128)(2,1)} %param.19) | copy-start | bytes 589828
  347.2 260.5 %copy-start.5 = (bf16[2,2,48,16]{2,3,1,0:T(8,128)(2,1)S(1)}, bf16[2,2,48,16]{2,3,1,0:T(8,128)(2,1)}, u32[]{:S(2)}) copy-start(bf16[2,2,48,16]{2,3,1,0:T(8,128)(2,1)} %param.21) | copy-start | bytes 18436
  347.2 306.5 %copy-start.2 = (bf16[1,72,1536]{2,1,0:T(8,128)(2,1)S(1)}, bf16[1,72,1536]{2,1,0:T(8,128)(2,1)}, u32[]{:S(2)}) copy-start(bf16[1,72,1536]{2,1,0:T(8,128)(2,1)} %param.13) | copy-start | bytes 663556
  347.2 307.9 %copy-start.9 = (f32[64]{0:T(128)S(1)}, f32[64]{0:T(128)}, u32[]{:S(2)}) copy-start(f32[64]{0:T(128)} %param.20) | copy-start | bytes 772
  355.0 5.9 copy-start.1
  371.1 5.9 copy-start.1
  387.3 5.9 copy-start.1
  403.4 5.9 copy-start.1
  419.5 5.9 copy-start.1
  435.6 5.9 copy-start.1
  451.8 5.9 copy-start.1
  467.9 5.9 copy-start.1
  484.0 5.9 copy-start.1
  500.1 5.9 copy-start.1
  516.3 5.9 copy-start.1
  532.4 5.9 copy-start.1
  548.5 5.9 copy-start.1
  564.7 5.9 copy-start.1
  580.8 5.9 copy-start.1
  596.9 5.9 copy-start.1
  605.5 61.5 %copy-start.7 = (bf16[432,384]{1,0:T(8,128)(2,1)S(1)}, bf16[432,384]{1,0:T(8,128)(2,1)}, u32[]{:S(2)}) copy-start(bf16[432,384]{1,0:T(8,128)(2,1)} %param.22) | copy-start | bytes 995332
  605.5 61.5 %copy-start.8 = (f32[384]{0:T(512)S(1)}, f32[384]{0:T(512)}, u32[]{:S(2)}) copy-start(f32[384]{0:T(512)} %param.23) | copy-start | bytes 4612
  607.5 111.1 %all-gather.12.cloned.1.call-start = ((), (), s32[]{:S(2)}) async-start(), calls=%async_computation.5 | async-start | bytes 1990656 | tf_op jit(solution)/shard_map/all_gather | solution.py:34
  654.9 66.1 %copy-start.3 = (bf16[72,1536]{1,0:T(8,128)(2,1)}, bf16[72,1536]{1,0:T(8,128)(2,1)S(1)}, u32[]{:S(2)}) copy-start(bf16[72,1536]{1,0:T(8,128)(2,1)S(1)} %get-tuple-element.107) | copy-start | bytes 663556
  655.8 8.0 %collective-permute-start = (bf16[5,1,48,16]{3,2,1,0:T(8,128)(2,1)S(1)}, bf16[5,1,48,16]{3,2,1,0:T(8,128)(2,1)S(1)}, u32[]{:S(2)}, u32[]{:S(2)}) collective-permute-start(bf16[5,1,48,16]{3,2,1,0:T(8,128)(2,1)S(1)} %get-tuple-element.141), channel_id=1, source_target_pairs={{0,1},{1,2},{2,3},{3,4},{4,5},{5,6},{6,7},{7,8},{8,9},{9,10},{10,1... | collective-permute-start | bytes 23048 | tf_op jit(solution)/shard_map/ppermute | solution.py:23
  657.7 7.9 %collective-permute-start.1 = (bf16[5,1,48,16]{3,2,1,0:T(8,128)(2,1)S(1)}, bf16[5,1,48,16]{3,2,1,0:T(8,128)(2,1)S(1)}, u32[]{:S(2)}, u32[]{:S(2)}) collective-permute-start(bf16[5,1,48,16]{3,2,1,0:T(8,128)(2,1)S(1)} %get-tuple-element.142), channel_id=1, source_target_pairs={{1,0},{2,1},{3,2},{4,3},{5,4},{6,5},{7,6},{8,7},{9,8},{10,9},{11,1... | collective-permute-start | bytes 23048 | tf_op jit(solution)/shard_map/ppermute | solution.py:25
Sparse Core Ops, SparseCore 0:
  12.8 51.1 all-gather.5
  68.2 105.7 all-gather.7
  176.8 102.6 all-gather.9
  607.6 46.1 reduce-scatter.1
  668.2 50.3 all-gather.11
